TPU v7x, 32 devices: a whole 2x2x4 slice. The times are simulated.
32 devices in a mesh: group: 2 (over x), dp: 16 (over z, y, core).
Axes of the slice: x: 2, y: 2, z: 4, core: 2. Of those that a mesh axis runs over, the one named last changes fastest.
Arguments:
- tokens: bfloat16 [4096, 8192], P(('group', 'dp')), parts along dimension 0, may hold values from -6 to 6
- grad_out: bfloat16 [4096, 8192], P(('group', 'dp')), parts along dimension 0, may hold values from -6 to 6
- down_factor_pool: bfloat16 [128, 8192, 128], P('group', 'dp'), parts along dimension 0, may hold values from -0.0625 to 0.0625
- up_pool: bfloat16 [128, 128, 8192], P('group', None, 'dp'), parts along dimension 0, may hold values from -0.25 to 0.25
- block_adapter: int32 [32], P('group'), parts along dimension 0, may hold values from 0 to 63, as said below
- counts: int32 [128], P('group'), parts along dimension 0, may hold values from 0 to 1024, as said below
- slot_map: int32 [128], P('group'), parts along dimension 0, may hold values from 0 to 63, each once
Outputs:
- adapter_output: bfloat16 [4096, 8192], P(('group', 'dp')), parts along dimension 0
- token_input_gradient: bfloat16 [4096, 8192], P(('group', 'dp')), parts along dimension 0
- down_factor_gradient: bfloat16 [128, 8192, 128], P('group', 'dp'), parts along dimension 0
- up_factor_gradient: bfloat16 [128, 128, 8192], P('group', None, 'dp'), parts along dimension 0
There are 2 independent parts, one for each index of `group`. A program takes and returns all parts, laid end to end along the dimension named above; each array names one. Nothing has to cross between parts.
Inputs may be any that keep to these rules, and one draw needn't show every extreme that they name: `block_adapter`: some block names adapter 0 and some adapter 64 - 1; no adapter is named by more than 8 blocks. `counts`: an adapter with k listed blocks has more than 128 * (k - 1) and at most 128 * k tokens; one with none has 0. `slot_map`: a permutation.
All inputs are finite; a program needn't handle non-finite values.
Results may differ from a plain program's by a relative error of at most 0.005.
Values may be sent and summed in bfloat16 or wider, within the bound.
A program may use at most 128 MiB of HBM per device.

v0:
```python
import jax
import jax.numpy as jnp
from jax import lax
from jax.sharding import PartitionSpec as P

BLOCK = 128


adapter_scale = 2.0


def block_tables(block_adapter, counts, slot_map, rows_per_block):
    blocks = block_adapter.shape[0]
    adapter_list = counts.shape[0]
    matches = block_adapter[:, None] == jnp.arange(adapter_list, dtype=jnp.int32)[None, :]
    block_count = jnp.sum(jnp.where(matches, counts[None, :], 0), axis=1)
    block_position = jnp.sum(jnp.where(matches, slot_map[None, :], 0), axis=1)
    same_adapter = block_adapter[:, None] == block_adapter[None, :]
    position = jnp.arange(blocks, dtype=jnp.int32)
    before = position[None, :] < position[:, None]
    ordinal = jnp.sum((same_adapter & before).astype(jnp.int32), axis=1)
    live_rows = jnp.clip(block_count - rows_per_block * ordinal, 0, rows_per_block)
    holder = slot_map[:, None] == jnp.arange(adapter_list, dtype=jnp.int32)[None, :]
    slot_count = jnp.sum(jnp.where(holder, counts[:, None], 0), axis=0)
    return (block_position, live_rows, slot_count)


def per_slot(chooser, pieces):
    blocks = pieces.shape[0]
    summed = jnp.dot(
        chooser,
        pieces.reshape(blocks, -1),
        precision=lax.Precision.HIGHEST,
        preferred_element_type=jnp.float32,
    )
    return summed.reshape((chooser.shape[0],) + pieces.shape[1:])


def body(tokens, grad_out, down_factor_pool, up_pool, block_adapter, counts, slot_map):
    token_per_device, model_width = tokens.shape
    rows_per_block = BLOCK
    block_per_device = token_per_device // rows_per_block
    adapter_list, segment_width, adapter_rank = down_factor_pool.shape
    block_position, live_rows, slot_count = block_tables(
        block_adapter, counts, slot_map, rows_per_block
    )
    first_block = lax.axis_index("dp") * block_per_device
    own_live = lax.dynamic_slice_in_dim(live_rows, first_block, block_per_device)
    active_row_mask = (
        (jnp.arange(rows_per_block, dtype=jnp.int32)[None, :] < own_live[:, None])
        .astype(jnp.float32)
        .reshape(token_per_device, 1)
    )
    columns = None
    columns = lax.all_to_all(tokens, "dp", split_axis=1, concat_axis=0, tiled=True)
    down_sel = down_factor_pool[block_position]
    up_turned = jnp.swapaxes(up_pool, 1, 2)
    up_sel = up_turned[block_position]
    down_full, up_full = (
        lax.all_to_all(down_sel, "dp", split_axis=0, concat_axis=1, tiled=True),
        lax.all_to_all(up_sel, "dp", split_axis=0, concat_axis=1, tiled=True),
    )
    x_blocks = tokens.reshape(block_per_device, rows_per_block, model_width)
    count_of_rows = token_per_device * lax.axis_size("dp")
    token_slab = columns.reshape(count_of_rows // rows_per_block, rows_per_block, segment_width)
    summed_low = lax.psum_scatter(
        jnp.einsum(
            "kbd,kdr->kbr", token_slab, down_sel, preferred_element_type=jnp.float32
        ).reshape(count_of_rows, adapter_rank),
        "dp",
        scatter_dimension=0,
        tiled=True,
    )
    projected_rows = (summed_low * active_row_mask).astype(jnp.bfloat16)
    reduced_blocks = projected_rows.reshape(block_per_device, rows_per_block, adapter_rank)
    adapter_output = (
        (
            adapter_scale
            * jnp.einsum(
                "kbr,kdr->kbd", reduced_blocks, up_full, preferred_element_type=jnp.float32
            )
        )
        .astype(jnp.bfloat16)
        .reshape(token_per_device, model_width)
    )
    g_blocks = grad_out.reshape(block_per_device, rows_per_block, model_width)
    backward_total = jnp.einsum(
        "kbd,kdr->kbr", g_blocks, up_full, preferred_element_type=jnp.float32
    ).reshape(token_per_device, adapter_rank)
    reduced_gradient = (adapter_scale * active_row_mask * backward_total).astype(jnp.bfloat16)
    gradient_block_list = reduced_gradient.reshape(block_per_device, rows_per_block, adapter_rank)
    chooser = (
        jnp.arange(adapter_list, dtype=jnp.int32)[:, None] == block_position[None, :]
    ).astype(jnp.float32)
    inverse = 1.0 / jnp.maximum(slot_count, 1).astype(jnp.float32)
    sum_b = None
    second_term = None
    second_term = adapter_scale * jnp.einsum(
        "kbd,kbr->kdr", g_blocks, reduced_blocks, preferred_element_type=jnp.float32
    )
    incoming_gradient = (
        jnp.einsum(
            "kbr,kdr->kbd", gradient_block_list, down_full, preferred_element_type=jnp.float32
        )
        .astype(jnp.bfloat16)
        .reshape(token_per_device, model_width)
    )
    term_a = jnp.einsum(
        "kbd,kbr->kdr", x_blocks, gradient_block_list, preferred_element_type=jnp.float32
    )
    got_a, got_b = (
        lax.all_to_all(term_a, "dp", split_axis=1, concat_axis=0, tiled=True),
        lax.all_to_all(second_term, "dp", split_axis=1, concat_axis=0, tiled=True),
    )
    sum_b = per_slot(chooser, got_b)
    sum_a = per_slot(chooser, got_a)
    down_factor_gradient = (sum_a * inverse[:, None, None]).astype(jnp.bfloat16)
    up_factor_gradient = jnp.swapaxes(sum_b * inverse[:, None, None], 1, 2).astype(jnp.bfloat16)
    return (adapter_output, incoming_gradient, down_factor_gradient, up_factor_gradient)


def solution(mesh):
    placed = (
        P(("group", "dp"), None),
        P(("group", "dp"), None),
        P("group", "dp", None),
        P("group", None, "dp"),
        P("group"),
        P("group"),
        P("group"),
    )
    return jax.shard_map(
        body,
        mesh=mesh,
        in_specs=placed,
        out_specs=(
            P(("group", "dp"), None),
            P(("group", "dp"), None),
            P("group", "dp", None),
            P("group", None, "dp"),
        ),
        check_vma=False,
    )
```

profile of v0, /device:TPU:29, one launch (start us, length us, event | category | flops | bytes accessed | tf_op | source)
XLA Modules:
  0.0 446.0 jit_solution(644486089009776833)
XLA Ops:
  8.2 5.5 %gather_fusion = bf16[16,512,128]{2,1,0:T(8,128)(2,1)} fusion(bf16[64,512,128]{2,1,0:T(8,128)(2,1)} %param.9, s32[1024]{0:T(1024)S(1)} %pad_clamp_fusion), kind=kCustom, calls=%fused_computation | custom fusion | bytes 4194368 | tf_op jit(solution)/shard_map/gather | solution.py:56
  13.7 6.3 %all-to-all-start.2 = ((bf16[16,512,128]{2,1,0:T(8,128)(2,1)}), bf16[16,512,128]{2,1,0:T(8,128)(2,1)}, u32[]{:S(2)}, u32[]{:S(2)}) async-start(bf16[16,512,128]{2,1,0:T(8,128)(2,1)} %gather_fusion), calls=%async_computation.3 | async-start | bytes 4194304 | tf_op jit(solution)/shard_map/all_to_all | solution.py:60
  20.1 11.9 %copy.41 = bf16[64,128,512]{1,2,0:T(8,128)(2,1)} copy(bf16[64,128,512]{2,1,0:T(8,128)(2,1)} %param.10) | data formatting | bytes 16777216 | tf_op args[3]
  32.0 5.5 %gather_fusion.1 = bf16[16,512,128]{2,1,0:T(8,128)(2,1)} fusion(bf16[64,512,128]{2,1,0:T(8,128)(2,1)} %bitcast.56, s32[1024]{0:T(1024)S(1)} %pad_clamp_fusion), kind=kCustom, calls=%fused_computation.1 | custom fusion | bytes 4194368 | tf_op jit(solution)/shard_map/gather | solution.py:58
  37.5 29.1 %all-to-all-done.2 = bf16[16,512,128]{2,1,0:T(8,128)(2,1)} async-done(((bf16[16,512,128]{2,1,0:T(8,128)(2,1)}), bf16[16,512,128]{2,1,0:T(8,128)(2,1)}, u32[]{:S(2)}, u32[]{:S(2)}) %all-to-all-start.2) | async-done | bytes 2097184 | tf_op jit(solution)/shard_map/all_to_all | solution.py:60
  66.6 5.9 %all-to-all-start.1 = ((bf16[16,512,128]{2,1,0:T(8,128)(2,1)}), bf16[16,512,128]{2,1,0:T(8,128)(2,1)}, u32[]{:S(2)}, u32[]{:S(2)}) async-start(bf16[16,512,128]{2,1,0:T(8,128)(2,1)} %gather_fusion.1), calls=%async_computation.2 | async-start | bytes 4194304 | tf_op jit(solution)/shard_map/all_to_all | solution.py:61
  72.5 4.1 copy.39
  80.5 38.6 %all-to-all-done.1 = bf16[16,512,128]{2,1,0:T(8,128)(2,1)} async-done(((bf16[16,512,128]{2,1,0:T(8,128)(2,1)}), bf16[16,512,128]{2,1,0:T(8,128)(2,1)}, u32[]{:S(2)}, u32[]{:S(2)}) %all-to-all-start.1) | async-done | bytes 2097184 | tf_op jit(solution)/shard_map/all_to_all | solution.py:61
  119.1 5.9 %all-to-all-start = ((bf16[128,16,512]{2,0,1:T(8,128)(2,1)}), bf16[128,16,512]{2,0,1:T(8,128)(2,1)}, u32[]{:S(2)}, u32[]{:S(2)}) async-start(bf16[128,16,512]{2,0,1:T(8,128)(2,1)} %copy.40), calls=%async_computation | async-start | bytes 4194304 | tf_op jit(solution)/shard_map/all_to_all | solution.py:55
  131.5 9.6 %copy.42 = f32[1,8192,128]{2,0,1:T(1,128)} copy(f32[1,8192,128]{1,2,0:T(8,128)} %convolution_bitcast_fusion) | data formatting | bytes 8388608 | tf_op jit(solution)/shard_map/kbd,kbr->kdr/dot_general | solution.py:108
  141.1 30.4 %all-to-all-done = bf16[128,16,512]{2,0,1:T(8,128)(2,1)} async-done(((bf16[128,16,512]{2,0,1:T(8,128)(2,1)}), bf16[128,16,512]{2,0,1:T(8,128)(2,1)}, u32[]{:S(2)}, u32[]{:S(2)}) %all-to-all-start) | async-done | bytes 2097184 | tf_op jit(solution)/shard_map/all_to_all | solution.py:55
  171.5 5.9 %all-to-all-start.3 = ((f32[1,8192,128]{2,0,1:T(1,128)}), f32[1,8192,128]{2,0,1:T(1,128)}, u32[]{:S(2)}, u32[]{:S(2)}) async-start(f32[1,8192,128]{2,0,1:T(1,128)} %copy.42), calls=%async_computation.4 | async-start | bytes 8388608 | tf_op jit(solution)/shard_map/all_to_all | solution.py:112
  182.0 82.5 %reduce-scatter.2.cloned.1.call-done = f32[128,128]{1,0:T(8,128)} async-done(((f32[2048,128]{1,0:T(8,128)}), f32[128,128]{1,0:T(8,128)}) %reduce-scatter.2.cloned.1.call-update) | async-done | bytes 65552 | tf_op jit(solution)/shard_map/reduce_scatter | solution.py:66
  268.2 9.7 %copy.44 = f32[1,8192,128]{2,0,1:T(1,128)} copy(f32[1,8192,128]{1,2,0:T(8,128)} %fusion) | data formatting | bytes 8388608 | tf_op jit(solution)/shard_map/mul | solution.py:98
  277.8 7.6 %all-to-all-start.4 = ((f32[1,8192,128]{2,0,1:T(1,128)}), f32[1,8192,128]{2,0,1:T(1,128)}, u32[]{:S(2)}, u32[]{:S(2)}) async-start(f32[1,8192,128]{2,0,1:T(1,128)} %copy.44), calls=%async_computation.5 | async-start | bytes 8388608 | tf_op jit(solution)/shard_map/all_to_all | solution.py:113
  293.4 34.2 %reduce.6 = f32[8192,128]{1,0:T(8,128)} reduce(f32[1,8192,128]{2,0,1:T(1,128)} %all-to-all-done.3, f32[]{:T(128)} %broadcast.90), dimensions={0}, to_apply=%all_to_all.20.reduce_sub_computation.3 | reduce | bytes 8388612 | tf_op jit(solution)/shard_map/all_to_all | solution.py:112
  327.6 4.0 reshape.137
  331.6 11.3 %multiply_convert_fusion.1 = bf16[64,512,128]{2,0,1:T(8,128)(2,1)} fusion(f32[64]{0:T(128)S(1)} %convert_divide_fusion, s32[16]{0:T(128)S(1)} %get-tuple-element.25, f32[16,65536]{1,0:T(8,128)} %reshape.137), kind=kOutput, calls=%fused_computation.3 | convolution fusion | flops 813696000 | bytes 12583232 | tf_op jit(solution)/shard_map/dot_general | solution.py:30
  342.9 12.2 %copy.46 = bf16[64,512,128]{2,1,0:T(8,128)(2,1)} copy(bf16[64,512,128]{2,0,1:T(8,128)(2,1)} %multiply_convert_fusion.1) | data formatting | bytes 16777216
  355.1 21.8 %all-to-all-done.4 = f32[1,8192,128]{2,0,1:T(1,128)} async-done(((f32[1,8192,128]{2,0,1:T(1,128)}), f32[1,8192,128]{2,0,1:T(1,128)}, u32[]{:S(2)}, u32[]{:S(2)}) %all-to-all-start.4) | async-done | bytes 4194336 | tf_op jit(solution)/shard_map/all_to_all | solution.py:113
  376.9 34.2 %reduce.7 = f32[8192,128]{1,0:T(8,128)} reduce(f32[1,8192,128]{2,0,1:T(1,128)} %all-to-all-done.4, f32[]{:T(128)} %broadcast.90), dimensions={0}, to_apply=%all_to_all.21.reduce_sub_computation.3 | reduce | bytes 8388612 | tf_op jit(solution)/shard_map/all_to_all | solution.py:113
  411.1 3.9 reshape.138
  415.0 11.2 %fusion.2 = bf16[64,128,512]{1,0,2:T(8,128)(2,1)} fusion(f32[64]{0:T(128)S(1)} %convert_divide_fusion, s32[16]{0:T(128)S(1)} %get-tuple-element.25, f32[16,65536]{1,0:T(8,128)} %reshape.138), kind=kOutput, calls=%fused_computation.10 | convolution fusion | flops 813696000 | bytes 12583232 | tf_op jit(solution)/shard_map/dot_general | solution.py:30
  426.2 13.0 %copy.47 = bf16[64,128,512]{2,1,0:T(8,128)(2,1)} copy(bf16[64,128,512]{1,0,2:T(8,128)(2,1)} %fusion.2) | data formatting | bytes 16777216
  (35 shorter events, 27.7 us)
Async XLA Ops:
  7.2 119.2 %copy-start = (bf16[128,8192]{1,0:T(8,128)(2,1)S(1)}, bf16[128,8192]{1,0:T(8,128)(2,1)}, u32[]{:S(2)}) copy-start(bf16[128,8192]{1,0:T(8,128)(2,1)} %param.8) | copy-start | bytes 6291460
  13.7 52.9 %all-to-all-start.2 = ((bf16[16,512,128]{2,1,0:T(8,128)(2,1)}), bf16[16,512,128]{2,1,0:T(8,128)(2,1)}, u32[]{:S(2)}, u32[]{:S(2)}) async-start(bf16[16,512,128]{2,1,0:T(8,128)(2,1)} %gather_fusion), calls=%async_computation.3 | async-start | bytes 4194304 | tf_op jit(solution)/shard_map/all_to_all | solution.py:60
  66.6 52.4 %all-to-all-start.1 = ((bf16[16,512,128]{2,1,0:T(8,128)(2,1)}), bf16[16,512,128]{2,1,0:T(8,128)(2,1)}, u32[]{:S(2)}, u32[]{:S(2)}) async-start(bf16[16,512,128]{2,1,0:T(8,128)(2,1)} %gather_fusion.1), calls=%async_computation.2 | async-start | bytes 4194304 | tf_op jit(solution)/shard_map/all_to_all | solution.py:61
  76.6 48.4 %copy-start.4 = (s32[16]{0:T(128)S(1)}, s32[16]{0:T(128)}, u32[]{:S(2)}) copy-start(s32[16]{0:T(128)} %param.11) | copy-start | bytes 196
  119.1 52.4 %all-to-all-start = ((bf16[128,16,512]{2,0,1:T(8,128)(2,1)}), bf16[128,16,512]{2,0,1:T(8,128)(2,1)}, u32[]{:S(2)}, u32[]{:S(2)}) async-start(bf16[128,16,512]{2,0,1:T(8,128)(2,1)} %copy.40), calls=%async_computation | async-start | bytes 4194304 | tf_op jit(solution)/shard_map/all_to_all | solution.py:55
  124.9 3.8 copy-start.2
  171.5 106.3 %all-to-all-start.3 = ((f32[1,8192,128]{2,0,1:T(1,128)}), f32[1,8192,128]{2,0,1:T(1,128)}, u32[]{:S(2)}, u32[]{:S(2)}) async-start(f32[1,8192,128]{2,0,1:T(1,128)} %copy.42), calls=%async_computation.4 | async-start | bytes 8388608 | tf_op jit(solution)/shard_map/all_to_all | solution.py:112
  177.4 87.1 %reduce-scatter.2.cloned.1.call-start = ((), (), s32[]{:S(2)}) async-start(), calls=%async_computation.6 | async-start | bytes 1114112 | tf_op jit(solution)/shard_map/reduce_scatter | solution.py:66
  277.8 7.6 %copy-start.5 = (s32[64]{0:T(128)S(1)}, s32[64]{0:T(128)}, u32[]{:S(2)}) copy-start(s32[64]{0:T(128)} %param.12) | copy-start | bytes 772
  277.8 7.6 %copy-start.6 = (s32[64]{0:T(128)S(1)}, s32[64]{0:T(128)}, u32[]{:S(2)}) copy-start(s32[64]{0:T(128)} %param.13) | copy-start | bytes 772
  277.8 99.0 %all-to-all-start.4 = ((f32[1,8192,128]{2,0,1:T(1,128)}), f32[1,8192,128]{2,0,1:T(1,128)}, u32[]{:S(2)}, u32[]{:S(2)}) async-start(f32[1,8192,128]{2,0,1:T(1,128)} %copy.44), calls=%async_computation.5 | async-start | bytes 8388608 | tf_op jit(solution)/shard_map/all_to_all | solution.py:113
  285.4 3.8 copy-start.3
  426.2 13.0 %copy-start.1 = (bf16[128,8192]{1,0:T(8,128)(2,1)S(1)}, bf16[128,8192]{1,0:T(8,128)(2,1)}, u32[]{:S(2)}) copy-start(bf16[128,8192]{1,0:T(8,128)(2,1)} %param.8) | copy-start | bytes 6291460
Sparse Core Ops, SparseCore 0:
  182.4 82.0 reduce-scatter.1
where the time goes:
time: 449 us; the launch traced here: 446 us
  waiting for transfers between devices  202 us (45%)
  local copies, waits for them, and re-layouts  84.5 us (19%)
  other arithmetic  71 us (16%)
  matrix products  42.4 us (9%)
  starting transfers between devices  31.6 us (7%)
  between operations  14.1 us (3%)
    reduce_scatter x1, waiting for transfers between devices, body(): lax.psum_scatter(jnp.einsum('kbd,kdr->kbr', token_slab, down_sel, preferr...  82.5 us
    unnamed x18, local copies, waits for them, and re-layouts  41.1 us
    all_to_all x1, waiting for transfers between devices, body(): lax.all_to_all(up_sel, 'dp', split_axis=0, concat_axis=1, tiled=True)  38.6 us
    all_to_all x1, other arithmetic, body(): lax.all_to_all(second_term, 'dp', split_axis=1, concat_axis=0, tiled=True)  34.2 us
    all_to_all x1, other arithmetic, body(): lax.all_to_all(term_a, 'dp', split_axis=1, concat_axis=0, tiled=True)  34.2 us
    all_to_all x1, waiting for transfers between devices, body(): lax.all_to_all(tokens, 'dp', split_axis=1, concat_axis=0, tiled=True)  30.4 us
    all_to_all x1, waiting for transfers between devices, body(): lax.all_to_all(down_sel, 'dp', split_axis=0, concat_axis=1, tiled=True)  29.1 us
    dot_general x2, matrix products, per_slot(): jnp.dot(chooser, pieces.reshape(blocks, -1), precision=lax.Precision.HIGH...  22.5 us
  transfers between devices with their start and end apart: 6, of which 5 were waited for; matrix products, arithmetic and copies ran while one was open for 29% of the time, Pallas kernels for 0%

commit v1 on v0

--- a/solution.py
+++ b/solution.py
@@ -1,6 +1,10 @@
+import functools
+
 import jax
 import jax.numpy as jnp
 from jax import lax
+from jax.experimental import pallas as pl
+from jax.experimental.pallas import tpu as pltpu
 from jax.sharding import PartitionSpec as P
 
 BLOCK = 128
@@ -36,7 +40,7 @@
     return summed.reshape((chooser.shape[0],) + pieces.shape[1:])
 
 
-def body(tokens, grad_out, down_factor_pool, up_pool, block_adapter, counts, slot_map):
+def collective_body(tokens, grad_out, down_factor_pool, up_pool, block_adapter, counts, slot_map):
     token_per_device, model_width = tokens.shape
     rows_per_block = BLOCK
     block_per_device = token_per_device // rows_per_block
@@ -119,6 +123,352 @@
     return (adapter_output, incoming_gradient, down_factor_gradient, up_factor_gradient)
 
 
+VMEM_BYTES = 48 * 1024 * 1024
+
+
+def pick_kernel(blocks, slots, down_pool, up_pool, down_sel, up_sel, sems):
+    def copies(k):
+        return (
+            pltpu.make_async_copy(down_pool.at[slots[k]], down_sel.at[k], sems.at[0, k]),
+            pltpu.make_async_copy(up_pool.at[slots[k]], up_sel.at[k], sems.at[1, k]),
+        )
+
+    @pl.loop(0, blocks)
+    def _(k):
+        for copy in copies(k):
+            copy.start()
+
+    @pl.loop(0, blocks)
+    def _(k):
+        for copy in copies(k):
+            copy.wait()
+
+
+def pick(block_position, down_pool, up_pool):
+    blocks = block_position.shape[0]
+    any_spec = pl.BlockSpec(memory_space=pl.ANY)
+    return pl.pallas_call(
+        functools.partial(pick_kernel, blocks),
+        grid_spec=pltpu.PrefetchScalarGridSpec(
+            num_scalar_prefetch=1,
+            grid=(1,),
+            in_specs=[any_spec] * 2,
+            out_specs=[any_spec] * 2,
+            scratch_shapes=[pltpu.SemaphoreType.DMA((2, blocks))],
+        ),
+        out_shape=[
+            jax.ShapeDtypeStruct((blocks,) + down_pool.shape[1:], jnp.bfloat16),
+            jax.ShapeDtypeStruct((blocks,) + up_pool.shape[1:], jnp.bfloat16),
+        ],
+        name="pick_factors",
+    )(block_position, down_pool, up_pool)
+
+
+def exchange_kernel(
+    n, seg,
+    tok, grd, down_sel, up_sel, mask,
+    out, tig, x_slab, g_slab, packs,
+    tok_v, grd_v, down_v, up_v, low_acc, grad_acc, mine, out_v, tig_v,
+    send, recv, own_send, fwd_send, pack_recv, local,
+):
+    me = lax.axis_index("dp")
+    half = n // 2
+    rows = mask.shape[0]
+    partner = lax.rem(me + half, n)
+    base = (me // half) * half
+
+    def columns(j):
+        return pl.ds(pl.multiple_of(j * seg, 128), seg)
+
+    def source(a, j):
+        if a == 0:
+            return down_sel.at[j]
+        if a == 1:
+            return up_sel.at[j]
+        return (tok if a == 2 else grd).at[:, columns(j)]
+
+    landing = (down_v, up_v, x_slab, g_slab)
+
+    def outgoing(a, peer):
+        return pltpu.make_async_remote_copy(
+            src_ref=source(a, peer), dst_ref=landing[a].at[me],
+            send_sem=send.at[a, peer], recv_sem=recv.at[a, me],
+            device_id={"dp": peer}, device_id_type=pl.DeviceIdType.MESH,
+        )
+
+    def incoming(a, j):
+        return pltpu.make_async_remote_copy(
+            src_ref=source(a, j), dst_ref=landing[a].at[j],
+            send_sem=send.at[a, j], recv_sem=recv.at[a, j],
+            device_id={"dp": j}, device_id_type=pl.DeviceIdType.MESH,
+        )
+
+    def own_pack(peer, origin):
+        return pltpu.make_async_remote_copy(
+            src_ref=mine, dst_ref=packs.at[origin],
+            send_sem=own_send.at[peer], recv_sem=pack_recv.at[origin],
+            device_id={"dp": peer}, device_id_type=pl.DeviceIdType.MESH,
+        )
+
+    def forwarded(peer):
+        return pltpu.make_async_remote_copy(
+            src_ref=packs.at[partner], dst_ref=packs.at[partner],
+            send_sem=fwd_send.at[peer], recv_sem=pack_recv.at[partner],
+            device_id={"dp": peer}, device_id_type=pl.DeviceIdType.MESH,
+        )
+
+    def near(d):
+        return base + lax.rem(me - base + d, half)
+
+    barrier = pltpu.get_barrier_semaphore()
+
+    @pl.loop(1, n)
+    def _(d):
+        pl.semaphore_signal(
+            barrier, inc=1, device_id={"dp": lax.rem(me + d, n)},
+            device_id_type=pl.DeviceIdType.MESH,
+        )
+
+    pl.semaphore_wait(barrier, n - 1)
+
+    @pl.loop(1, n)
+    def _(d):
+        peer = lax.rem(me + d, n)
+        outgoing(0, peer).start()
+        outgoing(1, peer).start()
+
+    @pl.loop(1, n)
+    def _(d):
+        outgoing(2, lax.rem(me + d, n)).start()
+
+    first = [
+        pltpu.make_async_copy(tok, tok_v, local.at[0]),
+        pltpu.make_async_copy(grd, grd_v, local.at[1]),
+        pltpu.make_async_copy(down_sel.at[me], down_v.at[me], local.at[2]),
+        pltpu.make_async_copy(up_sel.at[me], up_v.at[me], local.at[3]),
+    ]
+    later = [
+        pltpu.make_async_copy(tok.at[:, columns(me)], x_slab.at[me], local.at[4]),
+        pltpu.make_async_copy(grd.at[:, columns(me)], g_slab.at[me], local.at[5]),
+    ]
+    for copy in first + later:
+        copy.start()
+    for copy in first:
+        copy.wait()
+    low_acc[...] = jnp.zeros_like(low_acc)
+    grad_acc[...] = jnp.zeros_like(grad_acc)
+
+    def contract(j):
+        cols = columns(j)
+        low_acc[...] += jnp.dot(tok_v[:, cols], down_v[j], preferred_element_type=jnp.float32)
+        grad_acc[...] += lax.dot_general(
+            grd_v[:, cols], up_v[j], (((1,), (1,)), ((), ())),
+            preferred_element_type=jnp.float32,
+        )
+
+    contract(me)
+
+    @pl.loop(1, n)
+    def _(d):
+        j = lax.rem(me - d + n, n)
+        incoming(0, j).wait_recv()
+        incoming(1, j).wait_recv()
+        contract(j)
+
+    mine[:rows, :] = (low_acc[...] * mask[...]).astype(jnp.bfloat16)
+    mine[rows:, :] = (adapter_scale * mask[...] * grad_acc[...]).astype(jnp.bfloat16)
+    own = pltpu.make_async_copy(mine, packs.at[me], local.at[6])
+    own.start()
+    own_pack(partner, me).start()
+
+    @pl.loop(1, half)
+    def _(d):
+        own_pack(near(d), me).start()
+
+    @pl.loop(1, n)
+    def _(d):
+        outgoing(3, lax.rem(me + d, n)).start()
+
+    @pl.loop(0, n)
+    def _(j):
+        cols = columns(j)
+        out_v[:, cols] = (
+            adapter_scale
+            * jnp.dot(mine[:rows, :], up_v[j], preferred_element_type=jnp.float32)
+        ).astype(jnp.bfloat16)
+        tig_v[:, cols] = lax.dot_general(
+            mine[rows:, :], down_v[j], (((1,), (1,)), ((), ())),
+            preferred_element_type=jnp.float32,
+        ).astype(jnp.bfloat16)
+
+    results = [
+        pltpu.make_async_copy(out_v, out, local.at[7]),
+        pltpu.make_async_copy(tig_v, tig, local.at[8]),
+    ]
+    for copy in results:
+        copy.start()
+    own_pack(partner, partner).wait_recv()
+
+    @pl.loop(1, half)
+    def _(d):
+        forwarded(near(d)).start()
+
+    @pl.loop(1, half)
+    def _(d):
+        peer = near(d)
+        own_pack(peer, peer).wait_recv()
+        own_pack(peer, lax.rem(peer + half, n)).wait_recv()
+
+    for copy in later + [own] + results:
+        copy.wait()
+
+    @pl.loop(1, half)
+    def _(d):
+        own_pack(near(d), me).wait_send()
+        forwarded(near(d)).wait_send()
+
+    own_pack(partner, me).wait_send()
+
+    @pl.loop(1, n)
+    def _(d):
+        peer = lax.rem(me + d, n)
+        for a in range(4):
+            outgoing(a, peer).wait_send()
+        incoming(2, peer).wait_recv()
+        incoming(3, peer).wait_recv()
+
+
+def exchange(n, tokens, grad_out, down_sel, up_sel, mask):
+    rows, width = tokens.shape
+    seg, rank = down_sel.shape[1:]
+    any_spec = pl.BlockSpec(memory_space=pl.ANY)
+    sems = pltpu.SemaphoreType.DMA
+    bf16, f32 = jnp.bfloat16, jnp.float32
+    return pl.pallas_call(
+        functools.partial(exchange_kernel, n, seg),
+        in_specs=[any_spec] * 4 + [pl.BlockSpec(memory_space=pltpu.VMEM)],
+        out_specs=[any_spec] * 5,
+        out_shape=[
+            jax.ShapeDtypeStruct((rows, width), bf16),
+            jax.ShapeDtypeStruct((rows, width), bf16),
+            jax.ShapeDtypeStruct((n, rows, seg), bf16),
+            jax.ShapeDtypeStruct((n, rows, seg), bf16),
+            jax.ShapeDtypeStruct((n, 2 * rows, rank), bf16),
+        ],
+        scratch_shapes=[
+            pltpu.VMEM((rows, width), bf16),
+            pltpu.VMEM((rows, width), bf16),
+            pltpu.VMEM((n, seg, rank), bf16),
+            pltpu.VMEM((n, rank, seg), bf16),
+            pltpu.VMEM((rows, rank), f32),
+            pltpu.VMEM((rows, rank), f32),
+            pltpu.VMEM((2 * rows, rank), bf16),
+            pltpu.VMEM((rows, width), bf16),
+            pltpu.VMEM((rows, width), bf16),
+            sems((4, n)),
+            sems((4, n)),
+            sems((n,)),
+            sems((n,)),
+            sems((n,)),
+            sems((9,)),
+        ],
+        compiler_params=pltpu.CompilerParams(
+            collective_id=0, has_side_effects=True, vmem_limit_bytes=VMEM_BYTES
+        ),
+        name="exchange",
+    )(tokens, grad_out, down_sel, up_sel, mask)
+
+
+def factor_kernel(per_step, order, start, inverse, x_slab, g_slab, packs, down_grad, up_grad):
+    rows = x_slab.shape[1]
+    first = pl.program_id(0) * per_step
+
+    @pl.loop(0, per_step)
+    def _(i):
+        slot = first + i
+        down_grad[i] = jnp.zeros(down_grad.shape[1:], down_grad.dtype)
+        up_grad[i] = jnp.zeros(up_grad.shape[1:], up_grad.dtype)
+        begin, end = start[slot], start[slot + 1]
+
+        @pl.when(end > begin)
+        def _():
+            def terms(position):
+                k = order[position]
+                pack = packs[k]
+                over_rows = (((0,), (0,)), ((), ()))
+                term_a = lax.dot_general(
+                    x_slab[k], pack[rows:], over_rows, preferred_element_type=jnp.float32
+                )
+                term_b = lax.dot_general(
+                    pack[:rows], g_slab[k], over_rows, preferred_element_type=jnp.float32
+                )
+                return term_a, term_b
+
+            def add(position, totals):
+                term_a, term_b = terms(position)
+                return totals[0] + term_a, totals[1] + term_b
+
+            total_a, total_b = lax.fori_loop(begin + 1, end, add, terms(begin))
+            scale = inverse[slot]
+            down_grad[i] = (total_a * scale).astype(down_grad.dtype)
+            up_grad[i] = (adapter_scale * total_b * scale).astype(up_grad.dtype)
+
+
+def factor_gradients(order, start, inverse, x_slab, g_slab, packs):
+    slots = inverse.shape[0]
+    _, rows, seg = x_slab.shape
+    rank = packs.shape[2]
+    per_step = 4 if slots % 4 == 0 else 1
+    whole = pl.BlockSpec(memory_space=pltpu.VMEM)
+    return pl.pallas_call(
+        functools.partial(factor_kernel, per_step),
+        grid_spec=pltpu.PrefetchScalarGridSpec(
+            num_scalar_prefetch=3,
+            grid=(slots // per_step,),
+            in_specs=[whole] * 3,
+            out_specs=[
+                pl.BlockSpec((per_step, seg, rank), lambda i, *_: (i, 0, 0)),
+                pl.BlockSpec((per_step, rank, seg), lambda i, *_: (i, 0, 0)),
+            ],
+        ),
+        out_shape=[
+            jax.ShapeDtypeStruct((slots, seg, rank), jnp.bfloat16),
+            jax.ShapeDtypeStruct((slots, rank, seg), jnp.bfloat16),
+        ],
+        compiler_params=pltpu.CompilerParams(vmem_limit_bytes=VMEM_BYTES),
+        name="factor_gradients",
+    )(order, start, inverse, x_slab, g_slab, packs)
+
+
+def kernel_body(tokens, grad_out, down_factor_pool, up_pool, block_adapter, counts, slot_map):
+    n = lax.axis_size("dp")
+    slots, _, rank = down_factor_pool.shape
+    block_position, live_rows, slot_count = block_tables(block_adapter, counts, slot_map, BLOCK)
+    own_live = lax.dynamic_slice_in_dim(live_rows, lax.axis_index("dp"), 1)
+    mask = (
+        lax.broadcasted_iota(jnp.int32, (BLOCK, rank), 0) < own_live[:, None]
+    ).astype(jnp.float32)
+    down_sel, up_sel = pick(block_position, down_factor_pool, up_pool)
+    out, tig, x_slab, g_slab, packs = exchange(n, tokens, grad_out, down_sel, up_sel, mask)
+    index = jnp.arange(n, dtype=jnp.int32)
+    keys = block_position * n + index
+    rank_of = jnp.sum((keys[None, :] < keys[:, None]).astype(jnp.int32), axis=1)
+    order = jnp.sum(jnp.where(rank_of[None, :] == index[:, None], index[None, :], 0), axis=1)
+    slot_ids = jnp.arange(slots + 1, dtype=jnp.int32)
+    start = jnp.sum((block_position[None, :] < slot_ids[:, None]).astype(jnp.int32), axis=1)
+    inverse = 1.0 / jnp.maximum(slot_count, 1).astype(jnp.float32)
+    down_grad, up_grad = factor_gradients(order, start, inverse, x_slab, g_slab, packs)
+    return out, tig, down_grad, up_grad
+
+
+def body(tokens, *rest):
+    n = lax.axis_size("dp")
+    seg = rest[1].shape[1]
+    if tokens.shape[0] == BLOCK and seg % 128 == 0 and n % 2 == 0:
+        return kernel_body(tokens, *rest)
+    return collective_body(tokens, *rest)
+
+
 def solution(mesh):
     placed = (
         P(("group", "dp"), None),

time: 449 us -> 348 us (0.78)
  Pallas kernels: 0 us -> 337 us
  waiting for transfers between devices: 202 us -> 0 us
  local copies, waits for them, and re-layouts: 84.5 us -> 6.48 us
  other arithmetic: 71 us -> 3.61 us
  matrix products: 42.4 us -> 0 us
  starting transfers between devices: 31.6 us -> 0 us
  between operations: 14.1 us -> 0.7 us
    pallas_call x0 -> x3, Pallas kernels: none -> 337 us  [the longest x1 194 us: exchange(): pl.pallas_call(functools.partial(exchange_kernel, n, seg), in_specs=[any_...]
    all_to_all x5 -> x0, waiting for transfers between devices: 120 us -> none  [the longest x1 38.6 us: body(): lax.all_to_all(up_sel, 'dp', split_axis=0, concat_axis=1, tiled=True)]
    reduce_scatter x1 -> x0, waiting for transfers between devices: 82.5 us -> none  [body(): lax.psum_scatter(jnp.einsum('kbd,kdr->kbr', token_slab, down_sel, preferr...]
    all_to_all x2 -> x0, other arithmetic: 68.4 us -> none  [the longest x1 34.2 us: body(): lax.all_to_all(second_term, 'dp', split_axis=1, concat_axis=0, tiled=True)]
    dot_general x8 -> x0, matrix products: 42.4 us -> none  [the longest x2 22.5 us: per_slot(): jnp.dot(chooser, pieces.reshape(blocks, -1), precision=lax.Precision.HIGH...]
    unnamed x18 -> x8, local copies, waits for them, and re-layouts: 41.1 us -> 5.82 us
    all_to_all x5 -> x0, starting transfers between devices: 31.5 us -> none  [the longest x1 7.59 us: body(): lax.all_to_all(second_term, 'dp', split_axis=1, concat_axis=0, tiled=True)]
    gather x2 -> x0, local copies, waits for them, and re-layouts: 11 us -> none  [the longest x1 5.52 us: body(): down_sel = down_factor_pool[block_position]]
  transfers between devices with their start and end apart: 6 -> 0, of which waited for: 5 -> 0; matrix products, arithmetic and copies ran while one was open for 29% -> 0% of each run, Pallas kernels for 0% -> 0%
where the time goes in v1:
time: 348 us
  Pallas kernels  337 us (97%)
  local copies, waits for them, and re-layouts  6.48 us (2%)
  other arithmetic  3.61 us (1%)
    pallas_call x1, Pallas kernels, exchange(): pl.pallas_call(functools.partial(exchange_kernel, n, seg), in_specs=[any_...  194 us
    pallas_call x1, Pallas kernels, pick(): pl.pallas_call(functools.partial(pick_kernel, blocks), grid_spec=pltpu.Pr...  129 us
    pallas_call x1, Pallas kernels, factor_gradients(): pl.pallas_call(functools.partial(factor_kernel, per_step), grid_spec=pltp...  13.8 us

profile of v1, /device:TPU:29, one launch (start us, length us, event | category | flops | bytes accessed | tf_op | source)
XLA Modules:
  0.0 347.5 jit_solution(6743032434761929622)
XLA Ops:
  0.6 0.9 convert_reduce_fusion.2
  1.5 0.8 select_reduce_fusion
  2.3 0.9 select_reduce_fusion.2
  3.2 0.0 copy-start.2
  3.2 0.6 dynamic_slice.3
  3.8 0.2 convert_reduce_fusion.1
  4.0 0.1 select_reduce_fusion.1.order
  4.1 0.7 compare_convert_fusion
  4.8 0.1 convert_reduce_fusion.start
  4.9 0.1 iota.31.mask
  4.9 0.0 copy-done.2
  4.9 129.1 %pick_factors.1 = (bf16[16,512,128]{2,1,0:T(8,128)(2,1)}, bf16[16,128,512]{2,1,0:T(8,128)(2,1)}) custom-call(s32[16]{0:T(128)} %copy-done.2, bf16[64,512,128]{2,1,0:T(8,128)(2,1)} %down_pool.1, bf16[64,128,512]{2,1,0:T(8,128)(2,1)} %up_pool.1), custom_call_target="tpu_custom_call" | custom-call | tf_op jit(solution)/shard_map/pick_factors/pallas_call | solution.py:150
  134.1 193.8 %exchange.1 = (bf16[128,8192]{1,0:T(8,128)(2,1)S(1)}, bf16[128,8192]{1,0:T(8,128)(2,1)S(1)}, bf16[16,128,512]{2,1,0:T(8,128)(2,1)}, bf16[16,128,512]{2,1,0:T(8,128)(2,1)}, bf16[16,256,128]{2,1,0:T(8,128)(2,1)S(1)}) custom-call(bf16[128,8192]{1,0:T(8,128)(2,1)} %tok.1, bf16[128,8192]{1,0:T(8,128)(2,1)} %grd.1, ...), custom_call_target="tpu_custom_call" | custom-call | tf_op jit(solution)/shard_map/exchange/pallas_call | solution.py:347
  327.9 0.0 copy-start
  327.9 1.6 copy-done
  329.5 0.0 copy-start.1
  329.5 1.6 copy-done.1
  331.1 13.8 %factor_gradients.1 = (bf16[64,512,128]{2,1,0:T(8,128)(2,1)}, bf16[64,128,512]{2,1,0:T(8,128)(2,1)}) custom-call(s32[16]{0:T(128)S(1)} %select_reduce_fusion.1.order, s32[65]{0:T(128)S(1)} %convert_reduce_fusion.start, f32[64]{0:T(128)S(1)} %convert_divide_fusion.inverse, bf16[16,128,512]{2,1,0:T(8,128)(2,1)S(1)} %copy-done, ...), custom_call_target="tpu_custom_call" | custom-call | tf_op jit(solution)/shard_map/factor_gradients/pallas_call | solution.py:423
  344.9 1.3 copy.13
  346.2 1.3 copy.14
  (2 shorter events, 0.0 us)
Async XLA Ops:
  3.2 1.7 copy-start.2
  327.9 1.6 copy-start
  329.5 1.6 copy-start.1

commit v2 on v1

--- a/solution.py
+++ b/solution.py
@@ -123,52 +123,93 @@
     return (adapter_output, incoming_gradient, down_factor_gradient, up_factor_gradient)
 
 
-VMEM_BYTES = 48 * 1024 * 1024
-
-
-def pick_kernel(blocks, slots, down_pool, up_pool, down_sel, up_sel, sems):
-    def copies(k):
+MIB = 1024 * 1024
+
+
+def pick_kernel(
+    n, slots,
+    block_adapter, counts, slot_map, down_pool, up_pool,
+    down_sel, up_sel, mask, order, start,
+    held, ordinal, get,
+):
+    def slot_of(k):
+        return slot_map[block_adapter[k]]
+
+    def gets(k):
         return (
-            pltpu.make_async_copy(down_pool.at[slots[k]], down_sel.at[k], sems.at[0, k]),
-            pltpu.make_async_copy(up_pool.at[slots[k]], up_sel.at[k], sems.at[1, k]),
-        )
-
-    @pl.loop(0, blocks)
+            pltpu.make_async_copy(down_pool.at[slot_of(k)], down_sel.at[k], get.at[0, k]),
+            pltpu.make_async_copy(up_pool.at[slot_of(k)], up_sel.at[k], get.at[1, k]),
+        )
+
+    @pl.loop(0, n)
     def _(k):
-        for copy in copies(k):
+        for copy in gets(k):
             copy.start()
 
-    @pl.loop(0, blocks)
+    @pl.loop(0, slots)
+    def _(s):
+        held[s] = 0
+
+    @pl.loop(0, n)
     def _(k):
-        for copy in copies(k):
+        s = slot_of(k)
+        ordinal[k] = held[s]
+        held[s] = held[s] + 1
+
+    start[0] = 0
+
+    @pl.loop(0, slots)
+    def _(s):
+        start[s + 1] = start[s] + held[s]
+
+    @pl.loop(0, n)
+    def _(k):
+        order[start[slot_of(k)] + ordinal[k]] = k
+
+    me = lax.axis_index("dp")
+    rows = mask.shape[0]
+    live = counts[block_adapter[me]] - rows * ordinal[me]
+    row = lax.broadcasted_iota(jnp.int32, mask.shape, 0)
+    mask[...] = jnp.where(row < live, 1.0, 0.0).astype(jnp.float32)
+
+    @pl.loop(0, n)
+    def _(k):
+        for copy in gets(k):
             copy.wait()
 
 
-def pick(block_position, down_pool, up_pool):
-    blocks = block_position.shape[0]
-    any_spec = pl.BlockSpec(memory_space=pl.ANY)
+def pick(block_adapter, counts, slot_map, down_pool, up_pool):
+    n = block_adapter.shape[0]
+    slots, seg, rank = down_pool.shape
+    hbm = pl.BlockSpec(memory_space=pltpu.HBM)
+    vmem = pl.BlockSpec(memory_space=pltpu.VMEM)
+    smem = pl.BlockSpec(memory_space=pltpu.SMEM)
     return pl.pallas_call(
-        functools.partial(pick_kernel, blocks),
-        grid_spec=pltpu.PrefetchScalarGridSpec(
-            num_scalar_prefetch=1,
-            grid=(1,),
-            in_specs=[any_spec] * 2,
-            out_specs=[any_spec] * 2,
-            scratch_shapes=[pltpu.SemaphoreType.DMA((2, blocks))],
-        ),
+        functools.partial(pick_kernel, n, slots),
+        in_specs=[smem] * 3 + [hbm] * 2,
+        out_specs=[vmem] * 3 + [smem] * 2,
         out_shape=[
-            jax.ShapeDtypeStruct((blocks,) + down_pool.shape[1:], jnp.bfloat16),
-            jax.ShapeDtypeStruct((blocks,) + up_pool.shape[1:], jnp.bfloat16),
+            jax.ShapeDtypeStruct((n, seg, rank), jnp.bfloat16),
+            jax.ShapeDtypeStruct((n, rank, seg), jnp.bfloat16),
+            jax.ShapeDtypeStruct((BLOCK, rank), jnp.float32),
+            jax.ShapeDtypeStruct((n,), jnp.int32),
+            jax.ShapeDtypeStruct((slots + 1,), jnp.int32),
         ],
+        scratch_shapes=[
+            pltpu.SMEM((slots,), jnp.int32),
+            pltpu.SMEM((n,), jnp.int32),
+            pltpu.SemaphoreType.DMA((2, n)),
+        ],
+        compiler_params=pltpu.CompilerParams(vmem_limit_bytes=8 * MIB),
         name="pick_factors",
-    )(block_position, down_pool, up_pool)
+    )(block_adapter, counts, slot_map, down_pool, up_pool)
 
 
 def exchange_kernel(
     n, seg,
     tok, grd, down_sel, up_sel, mask,
     out, tig, x_slab, g_slab, packs,
-    tok_v, grd_v, down_v, up_v, low_acc, grad_acc, mine, out_v, tig_v,
+    tok_v, grd_v, down_v, up_v, low_acc, grad_acc, mine,
     send, recv, own_send, fwd_send, pack_recv, local,
 ):
     me = lax.axis_index("dp")
@@ -292,21 +333,15 @@
     @pl.loop(0, n)
     def _(j):
         cols = columns(j)
-        out_v[:, cols] = (
+        out[:, cols] = (
             adapter_scale
             * jnp.dot(mine[:rows, :], up_v[j], preferred_element_type=jnp.float32)
         ).astype(jnp.bfloat16)
-        tig_v[:, cols] = lax.dot_general(
+        tig[:, cols] = lax.dot_general(
             mine[rows:, :], down_v[j], (((1,), (1,)), ((), ())),
             preferred_element_type=jnp.float32,
         ).astype(jnp.bfloat16)
 
-    results = [
-        pltpu.make_async_copy(out_v, out, local.at[7]),
-        pltpu.make_async_copy(tig_v, tig, local.at[8]),
-    ]
-    for copy in results:
-        copy.start()
     own_pack(partner, partner).wait_recv()
 
     @pl.loop(1, half)
@@ -319,7 +354,7 @@
         own_pack(peer, peer).wait_recv()
         own_pack(peer, lax.rem(peer + half, n)).wait_recv()
 
-    for copy in later + [own] + results:
+    for copy in later + [own]:
         copy.wait()
 
     @pl.loop(1, half)
@@ -341,13 +376,14 @@
 def exchange(n, tokens, grad_out, down_sel, up_sel, mask):
     rows, width = tokens.shape
     seg, rank = down_sel.shape[1:]
-    any_spec = pl.BlockSpec(memory_space=pl.ANY)
+    hbm = pl.BlockSpec(memory_space=pltpu.HBM)
+    vmem = pl.BlockSpec(memory_space=pltpu.VMEM)
     sems = pltpu.SemaphoreType.DMA
     bf16, f32 = jnp.bfloat16, jnp.float32
     return pl.pallas_call(
         functools.partial(exchange_kernel, n, seg),
-        in_specs=[any_spec] * 4 + [pl.BlockSpec(memory_space=pltpu.VMEM)],
-        out_specs=[any_spec] * 5,
+        in_specs=[hbm] * 2 + [vmem] * 3,
+        out_specs=[vmem] * 2 + [vmem] * 3,
         out_shape=[
             jax.ShapeDtypeStruct((rows, width), bf16),
             jax.ShapeDtypeStruct((rows, width), bf16),
@@ -363,102 +399,124 @@
             pltpu.VMEM((rows, rank), f32),
             pltpu.VMEM((rows, rank), f32),
             pltpu.VMEM((2 * rows, rank), bf16),
-            pltpu.VMEM((rows, width), bf16),
-            pltpu.VMEM((rows, width), bf16),
             sems((4, n)),
             sems((4, n)),
             sems((n,)),
             sems((n,)),
             sems((n,)),
-            sems((9,)),
+            sems((7,)),
         ],
         compiler_params=pltpu.CompilerParams(
-            collective_id=0, has_side_effects=True, vmem_limit_bytes=VMEM_BYTES
+            collective_id=0, has_side_effects=True, vmem_limit_bytes=16 * MIB
         ),
         name="exchange",
     )(tokens, grad_out, down_sel, up_sel, mask)
 
 
-def factor_kernel(per_step, order, start, inverse, x_slab, g_slab, packs, down_grad, up_grad):
+def factor_kernel(
+    n, slots,
+    block_adapter, counts, slot_map, order, start, x_slab, g_slab, packs, out_in, tig_in,
+    out, tig, down_grad, up_grad,
+    no_down, no_up, acc_a, acc_b, sum_a, sum_b,
+    put, put_out,
+):
     rows = x_slab.shape[1]
-    first = pl.program_id(0) * per_step
-
-    @pl.loop(0, per_step)
+
+    def puts(slot, down_ref, up_ref):
+        return (
+            pltpu.make_async_copy(down_ref, down_grad.at[slot], put.at[0, slot]),
+            pltpu.make_async_copy(up_ref, up_grad.at[slot], put.at[1, slot]),
+        )
+
+    out_puts = (
+        pltpu.make_async_copy(out_in, out, put_out.at[0]),
+        pltpu.make_async_copy(tig_in, tig, put_out.at[1]),
+    )
+
+    for copy in out_puts:
+        copy.start()
+    no_down[...] = jnp.zeros_like(no_down)
+    no_up[...] = jnp.zeros_like(no_up)
+
+    @pl.loop(0, slots)
+    def _(slot):
+        @pl.when(start[slot] == start[slot + 1])
+        def _():
+            for copy in puts(slot, no_down, no_up):
+                copy.start()
+
+    @pl.loop(0, n)
     def _(i):
-        slot = first + i
-        down_grad[i] = jnp.zeros(down_grad.shape[1:], down_grad.dtype)
-        up_grad[i] = jnp.zeros(up_grad.shape[1:], up_grad.dtype)
-        begin, end = start[slot], start[slot + 1]
-
-        @pl.when(end > begin)
+        k = order[i]
+        slot = slot_map[block_adapter[k]]
+        over_rows = (((0,), (0,)), ((), ()))
+        term_a = lax.dot_general(
+            x_slab[k], packs[k, rows:, :], over_rows, preferred_element_type=jnp.float32
+        )
+        term_b = lax.dot_general(
+            packs[k, :rows, :], g_slab[k], over_rows, preferred_element_type=jnp.float32
+        )
+        fresh = i == start[slot]
+        acc_a[...] = jnp.where(fresh, term_a, acc_a[...] + term_a)
+        acc_b[...] = jnp.where(fresh, term_b, acc_b[...] + term_b)
+
+        @pl.when(i + 1 == start[slot + 1])
         def _():
-            def terms(position):
-                k = order[position]
-                pack = packs[k]
-                over_rows = (((0,), (0,)), ((), ()))
-                term_a = lax.dot_general(
-                    x_slab[k], pack[rows:], over_rows, preferred_element_type=jnp.float32
-                )
-                term_b = lax.dot_general(
-                    pack[:rows], g_slab[k], over_rows, preferred_element_type=jnp.float32
-                )
-                return term_a, term_b
-
-            def add(position, totals):
-                term_a, term_b = terms(position)
-                return totals[0] + term_a, totals[1] + term_b
-
-            total_a, total_b = lax.fori_loop(begin + 1, end, add, terms(begin))
-            scale = inverse[slot]
-            down_grad[i] = (total_a * scale).astype(down_grad.dtype)
-            up_grad[i] = (adapter_scale * total_b * scale).astype(up_grad.dtype)
-
-
-def factor_gradients(order, start, inverse, x_slab, g_slab, packs):
-    slots = inverse.shape[0]
-    _, rows, seg = x_slab.shape
+            held = jnp.maximum(counts[block_adapter[k]], 1)
+            scale = 1.0 / jnp.full((1, 128), held, jnp.int32).astype(jnp.float32)
+            sum_a[i] = (acc_a[...] * scale[:, :1]).astype(jnp.bfloat16)
+            sum_b[i] = (adapter_scale * acc_b[...] * scale[:, :1]).astype(jnp.bfloat16)
+            for copy in puts(slot, sum_a.at[i], sum_b.at[i]):
+                copy.start()
+
+    for copy in out_puts:
+        copy.wait()
+
+    @pl.loop(0, slots)
+    def _(slot):
+        for copy in puts(slot, no_down, no_up):
+            copy.wait()
+
+
+def factor_gradients(block_adapter, counts, slot_map, order, start, x_slab, g_slab, packs, out, tig):
+    slots = slot_map.shape[0]
+    n, rows, seg = x_slab.shape
     rank = packs.shape[2]
-    per_step = 4 if slots % 4 == 0 else 1
-    whole = pl.BlockSpec(memory_space=pltpu.VMEM)
+    hbm = pl.BlockSpec(memory_space=pltpu.HBM)
+    vmem = pl.BlockSpec(memory_space=pltpu.VMEM)
+    smem = pl.BlockSpec(memory_space=pltpu.SMEM)
+    bf16, f32 = jnp.bfloat16, jnp.float32
+    sems = pltpu.SemaphoreType.DMA
     return pl.pallas_call(
-        functools.partial(factor_kernel, per_step),
-        grid_spec=pltpu.PrefetchScalarGridSpec(
-            num_scalar_prefetch=3,
-            grid=(slots // per_step,),
-            in_specs=[whole] * 3,
-            out_specs=[
-                pl.BlockSpec((per_step, seg, rank), lambda i, *_: (i, 0, 0)),
-                pl.BlockSpec((per_step, rank, seg), lambda i, *_: (i, 0, 0)),
-            ],
-        ),
+        functools.partial(factor_kernel, n, slots),
+        in_specs=[smem] * 5 + [vmem] * 3 + [vmem] * 2,
+        out_specs=[hbm] * 4,
         out_shape=[
-            jax.ShapeDtypeStruct((slots, seg, rank), jnp.bfloat16),
-            jax.ShapeDtypeStruct((slots, rank, seg), jnp.bfloat16),
+            jax.ShapeDtypeStruct(out.shape, bf16),
+            jax.ShapeDtypeStruct(tig.shape, bf16),
+            jax.ShapeDtypeStruct((slots, seg, rank), bf16),
+            jax.ShapeDtypeStruct((slots, rank, seg), bf16),
         ],
-        compiler_params=pltpu.CompilerParams(vmem_limit_bytes=VMEM_BYTES),
+        scratch_shapes=[
+            pltpu.VMEM((seg, rank), bf16),
+            pltpu.VMEM((rank, seg), bf16),
+            pltpu.VMEM((seg, rank), f32),
+            pltpu.VMEM((rank, seg), f32),
+            pltpu.VMEM((n, seg, rank), bf16),
+            pltpu.VMEM((n, rank, seg), bf16),
+            sems((2, slots)),
+            sems((2,)),
+        ],
+        compiler_params=pltpu.CompilerParams(vmem_limit_bytes=24 * MIB),
         name="factor_gradients",
-    )(order, start, inverse, x_slab, g_slab, packs)
-
-
-def kernel_body(tokens, grad_out, down_factor_pool, up_pool, block_adapter, counts, slot_map):
+    )(block_adapter, counts, slot_map, order, start, x_slab, g_slab, packs, out, tig)
+
+
+def kernel_body(tokens, grad_out, down_factor_pool, up_pool, *tables):
     n = lax.axis_size("dp")
-    slots, _, rank = down_factor_pool.shape
-    block_position, live_rows, slot_count = block_tables(block_adapter, counts, slot_map, BLOCK)
-    own_live = lax.dynamic_slice_in_dim(live_rows, lax.axis_index("dp"), 1)
-    mask = (
-        lax.broadcasted_iota(jnp.int32, (BLOCK, rank), 0) < own_live[:, None]
-    ).astype(jnp.float32)
-    down_sel, up_sel = pick(block_position, down_factor_pool, up_pool)
+    down_sel, up_sel, mask, order, start = pick(*tables, down_factor_pool, up_pool)
     out, tig, x_slab, g_slab, packs = exchange(n, tokens, grad_out, down_sel, up_sel, mask)
-    index = jnp.arange(n, dtype=jnp.int32)
-    keys = block_position * n + index
-    rank_of = jnp.sum((keys[None, :] < keys[:, None]).astype(jnp.int32), axis=1)
-    order = jnp.sum(jnp.where(rank_of[None, :] == index[:, None], index[None, :], 0), axis=1)
-    slot_ids = jnp.arange(slots + 1, dtype=jnp.int32)
-    start = jnp.sum((block_position[None, :] < slot_ids[:, None]).astype(jnp.int32), axis=1)
-    inverse = 1.0 / jnp.maximum(slot_count, 1).astype(jnp.float32)
-    down_grad, up_grad = factor_gradients(order, start, inverse, x_slab, g_slab, packs)
-    return out, tig, down_grad, up_grad
+    return factor_gradients(*tables, order, start, x_slab, g_slab, packs, out, tig)
 
 
 def body(tokens, *rest):

time: 348 us -> 220 us (0.63)
  Pallas kernels: 337 us -> 211 us
  other arithmetic: 3.61 us -> 0 us
    pallas_call x3, Pallas kernels: 337 us -> 211 us  [the longest x1 193 us: exchange(): pl.pallas_call(functools.partial(exchange_kernel, n, seg), in_specs=[hbm]...]
    unnamed x8 -> x20, local copies, waits for them, and re-layouts: 5.82 us -> 8.75 us
where the time goes in v2:
time: 220 us
  Pallas kernels  211 us (96%)
  local copies, waits for them, and re-layouts  8.75 us (4%)
    pallas_call x1, Pallas kernels, exchange(): pl.pallas_call(functools.partial(exchange_kernel, n, seg), in_specs=[hbm]...  193 us
    unnamed x20, local copies, waits for them, and re-layouts  8.75 us
    pallas_call x1, Pallas kernels, factor_gradients(): pl.pallas_call(functools.partial(factor_kernel, n, slots), in_specs=[smem...  8.74 us
    pallas_call x1, Pallas kernels, pick(): pl.pallas_call(functools.partial(pick_kernel, n, slots), in_specs=[smem]...  8.44 us

profile of v2, /device:TPU:29, one launch (start us, length us, event | category | flops | bytes accessed | tf_op | source)
XLA Modules:
  0.0 220.1 jit_solution(11468877962881012254)
XLA Ops:
  0.6 0.0 copy-start
  0.6 3.4 %copy-done = bf16[64,512,128]{2,1,0:T(8,128)(2,1)S(1)} copy-done((bf16[64,512,128]{2,1,0:T(8,128)(2,1)S(1)}, bf16[64,512,128]{2,1,0:T(8,128)(2,1)}, u32[]{:S(2)}) %copy-start) | copy-done | bytes 8388632
  4.0 0.0 copy-start.1
  4.0 3.4 %copy-done.1 = bf16[64,128,512]{2,1,0:T(8,128)(2,1)S(1)} copy-done((bf16[64,128,512]{2,1,0:T(8,128)(2,1)S(1)}, bf16[64,128,512]{2,1,0:T(8,128)(2,1)}, u32[]{:S(2)}) %copy-start.1) | copy-done | bytes 8388632
  7.4 0.0 copy-start.4
  7.4 0.7 copy-done.4
  8.1 0.0 copy-start.6
  8.1 0.7 copy-done.6
  8.7 0.0 copy-start.8
  8.7 0.7 copy-done.8
  9.4 0.0 copy-start.2
  9.4 0.0 copy-start.3
  9.4 8.4 %pick_factors.1 = (bf16[16,512,128]{2,1,0:T(8,128)(2,1)S(1)}, bf16[16,128,512]{2,1,0:T(8,128)(2,1)S(1)}, f32[128,128]{1,0:T(8,128)S(1)}, s32[16]{0:T(128)S(1)}, s32[65]{0:T(128)S(1)}) custom-call(s32[16]{0:T(128)S(1)} %copy-done.4, s32[64]{0:T(128)S(1)} %copy-done.6, s32[64]{0:T(128)S(1)} %copy-done.8, bf16[64,512,128]{2,1,0:T(8,128)(2,1)S(1)} %copy-done, ...), custom_call_target="tpu_custom_call" | custom-call | tf_op jit(solution)/shard_map/pick_factors/pallas_call | solution.py:187
  17.8 0.0 copy-done.2
  17.8 0.0 copy-done.3
  17.8 0.0 copy-start.5
  17.9 0.0 copy-start.7
  17.9 0.0 copy-start.9
  17.9 193.5 %exchange.1 = (bf16[128,8192]{1,0:T(8,128)(2,1)S(1)}, bf16[128,8192]{1,0:T(8,128)(2,1)S(1)}, bf16[16,128,512]{2,1,0:T(8,128)(2,1)S(1)}, bf16[16,128,512]{2,1,0:T(8,128)(2,1)S(1)}, bf16[16,256,128]{2,1,0:T(8,128)(2,1)S(1)}) custom-call(bf16[128,8192]{1,0:T(8,128)(2,1)S(1)} %copy-done.2, bf16[128,8192]{1,0:T(8,128)(2,1)S(1)} %copy-done.3, ...), custom_call_target="tpu_custom_call" | custom-call | tf_op jit(solution)/shard_map/exchange/pallas_call | solution.py:383
  211.4 0.0 copy-done.5
  211.4 0.0 copy-done.7
  211.4 0.0 copy-done.9
  211.4 8.7 %factor_gradients.1 = (bf16[128,8192]{1,0:T(8,128)(2,1)}, bf16[128,8192]{1,0:T(8,128)(2,1)}, bf16[64,512,128]{2,1,0:T(8,128)(2,1)}, bf16[64,128,512]{2,1,0:T(8,128)(2,1)}) custom-call(s32[16]{0:T(128)S(1)} %copy-done.5, s32[64]{0:T(128)S(1)} %copy-done.7, s32[64]{0:T(128)S(1)} %copy-done.9, s32[16]{0:T(128)S(1)} %get-tuple-element.14.order, ...), custom_call_target="tpu_custom_call" | custom-call | tf_op jit(solution)/shard_map/factor_gradients/pallas_call | solution.py:490
Async XLA Ops:
  0.6 3.4 %copy-start = (bf16[64,512,128]{2,1,0:T(8,128)(2,1)S(1)}, bf16[64,512,128]{2,1,0:T(8,128)(2,1)}, u32[]{:S(2)}) copy-start(bf16[64,512,128]{2,1,0:T(8,128)(2,1)} %down_pool.1) | copy-start | bytes 25165828
  4.0 3.4 %copy-start.1 = (bf16[64,128,512]{2,1,0:T(8,128)(2,1)S(1)}, bf16[64,128,512]{2,1,0:T(8,128)(2,1)}, u32[]{:S(2)}) copy-start(bf16[64,128,512]{2,1,0:T(8,128)(2,1)} %up_pool.1) | copy-start | bytes 25165828
  7.4 0.7 copy-start.4
  8.1 0.7 copy-start.6
  8.7 0.7 copy-start.8
  9.4 8.5 %copy-start.2 = (bf16[128,8192]{1,0:T(8,128)(2,1)S(1)}, bf16[128,8192]{1,0:T(8,128)(2,1)}, u32[]{:S(2)}) copy-start(bf16[128,8192]{1,0:T(8,128)(2,1)} %tok.1) | copy-start | bytes 6291460
  9.4 8.5 %copy-start.3 = (bf16[128,8192]{1,0:T(8,128)(2,1)S(1)}, bf16[128,8192]{1,0:T(8,128)(2,1)}, u32[]{:S(2)}) copy-start(bf16[128,8192]{1,0:T(8,128)(2,1)} %grd.1) | copy-start | bytes 6291460
  17.8 193.5 %copy-start.5 = (s32[16]{0:T(128)S(1)}, s32[16]{0:T(128)}, u32[]{:S(2)}) copy-start(s32[16]{0:T(128)} %block_adapter.3) | copy-start | bytes 196
  17.9 193.5 %copy-start.7 = (s32[64]{0:T(128)S(1)}, s32[64]{0:T(128)}, u32[]{:S(2)}) copy-start(s32[64]{0:T(128)} %counts.3) | copy-start | bytes 772
  17.9 193.5 %copy-start.9 = (s32[64]{0:T(128)S(1)}, s32[64]{0:T(128)}, u32[]{:S(2)}) copy-start(s32[64]{0:T(128)} %slot_map.3) | copy-start | bytes 772

commit v3 on v2

--- a/solution.py
+++ b/solution.py
@@ -200,7 +200,7 @@
             pltpu.SMEM((n,), jnp.int32),
             pltpu.SemaphoreType.DMA((2, n)),
         ],
-        compiler_params=pltpu.CompilerParams(vmem_limit_bytes=8 * MIB),
+        compiler_params=pltpu.CompilerParams(vmem_limit_bytes=54 * MIB),
         name="pick_factors",
     )(block_adapter, counts, slot_map, down_pool, up_pool)
 
@@ -274,9 +274,11 @@
 
     @pl.loop(1, n)
     def _(d):
-        peer = lax.rem(me + d, n)
-        outgoing(0, peer).start()
-        outgoing(1, peer).start()
+        outgoing(0, lax.rem(me + d, n)).start()
+
+    @pl.loop(1, n)
+    def _(d):
+        outgoing(1, lax.rem(me + d, n)).start()
 
     @pl.loop(1, n)
     def _(d):

time: 220 us -> 212 us (0.964)
  local copies, waits for them, and re-layouts: 8.75 us -> 4.04 us
  Pallas kernels: 211 us -> 207 us
    unnamed x20, local copies, waits for them, and re-layouts: 8.75 us -> 4.04 us
    pallas_call x1, Pallas kernels: 8.44 us -> 5.75 us  [pick(): pl.pallas_call(functools.partial(pick_kernel, n, slots), in_specs=[smem]...]
where the time goes in v3:
time: 212 us
  Pallas kernels  207 us (98%)
  local copies, waits for them, and re-layouts  4.04 us (2%)
    pallas_call x1, Pallas kernels, exchange(): pl.pallas_call(functools.partial(exchange_kernel, n, seg), in_specs=[hbm]...  192 us
    pallas_call x1, Pallas kernels, factor_gradients(): pl.pallas_call(functools.partial(factor_kernel, n, slots), in_specs=[smem...  8.71 us
    pallas_call x1, Pallas kernels, pick(): pl.pallas_call(functools.partial(pick_kernel, n, slots), in_specs=[smem]...  5.75 us

profile of v3, /device:TPU:29, one launch (start us, length us, event | category | flops | bytes accessed | tf_op | source)
XLA Modules:
  0.0 211.6 jit_solution(10774318263830407220)
XLA Ops:
  0.6 0.0 copy-start.1
  0.6 0.0 copy-start
  0.7 5.8 %pick_factors.1 = (bf16[16,512,128]{2,1,0:T(8,128)(2,1)}, bf16[16,128,512]{2,1,0:T(8,128)(2,1)}, f32[128,128]{1,0:T(8,128)}, s32[16]{0:T(128)}, s32[65]{0:T(128)}) custom-call(s32[16]{0:T(128)} %block_adapter.3, s32[64]{0:T(128)} %counts.3, s32[64]{0:T(128)} %slot_map.3, bf16[64,512,128]{2,1,0:T(8,128)(2,1)} %down_pool.1, bf16[64,128,512]{2,1,0:T(8,128)(2,1)} %up_pool.1), custom_call_target="tpu_custom_call" | custom-call | tf_op jit(solution)/shard_map/pick_factors/pallas_call | solution.py:187
  6.4 0.0 copy-done.1
  6.4 0.0 copy-done
  6.4 0.0 copy-start.2
  6.4 1.6 copy-done.2
  8.0 0.0 copy-start.3
  8.0 1.6 copy-done.3
  9.6 0.0 copy-start.4
  9.6 0.8 copy-done.4
  10.5 0.0 copy-start.5
  10.5 0.0 copy-start.6
  10.5 0.0 copy-start.7
  10.5 0.0 copy-start.8
  10.5 0.0 copy-start.9
  10.5 192.3 %exchange.1 = (bf16[128,8192]{1,0:T(8,128)(2,1)S(1)}, bf16[128,8192]{1,0:T(8,128)(2,1)S(1)}, bf16[16,128,512]{2,1,0:T(8,128)(2,1)S(1)}, bf16[16,128,512]{2,1,0:T(8,128)(2,1)S(1)}, bf16[16,256,128]{2,1,0:T(8,128)(2,1)S(1)}) custom-call(bf16[128,8192]{1,0:T(8,128)(2,1)S(1)} %copy-done, bf16[128,8192]{1,0:T(8,128)(2,1)S(1)} %copy-done.1, ...), custom_call_target="tpu_custom_call" | custom-call | tf_op jit(solution)/shard_map/exchange/pallas_call | solution.py:385
  202.8 0.0 copy-done.5
  202.8 0.0 copy-done.6
  202.8 0.0 copy-done.7
  202.8 0.0 copy-done.8
  202.8 0.0 copy-done.9
  202.9 8.7 %factor_gradients.1 = (bf16[128,8192]{1,0:T(8,128)(2,1)}, bf16[128,8192]{1,0:T(8,128)(2,1)}, bf16[64,512,128]{2,1,0:T(8,128)(2,1)}, bf16[64,128,512]{2,1,0:T(8,128)(2,1)}) custom-call(s32[16]{0:T(128)S(1)} %copy-done.5, s32[64]{0:T(128)S(1)} %copy-done.6, s32[64]{0:T(128)S(1)} %copy-done.7, s32[16]{0:T(128)S(1)} %copy-done.8, s32[65]{0:T(128)S(1)} %copy-done.9, ...), custom_call_target="tpu_custom_call" | custom-call | tf_op jit(solution)/shard_map/factor_gradients/pallas_call | solution.py:492
Async XLA Ops:
  0.6 5.8 %copy-start.1 = (bf16[128,8192]{1,0:T(8,128)(2,1)S(1)}, bf16[128,8192]{1,0:T(8,128)(2,1)}, u32[]{:S(2)}) copy-start(bf16[128,8192]{1,0:T(8,128)(2,1)} %grd.1) | copy-start | bytes 6291460
  0.6 5.8 %copy-start = (bf16[128,8192]{1,0:T(8,128)(2,1)S(1)}, bf16[128,8192]{1,0:T(8,128)(2,1)}, u32[]{:S(2)}) copy-start(bf16[128,8192]{1,0:T(8,128)(2,1)} %tok.1) | copy-start | bytes 6291460
  6.4 1.6 copy-start.2
  8.0 1.6 copy-start.3
  9.6 0.8 copy-start.4
  10.5 192.3 %copy-start.5 = (s32[16]{0:T(128)S(1)}, s32[16]{0:T(128)}, u32[]{:S(2)}) copy-start(s32[16]{0:T(128)} %block_adapter.3) | copy-start | bytes 196
  10.5 192.4 %copy-start.6 = (s32[64]{0:T(128)S(1)}, s32[64]{0:T(128)}, u32[]{:S(2)}) copy-start(s32[64]{0:T(128)} %counts.3) | copy-start | bytes 772
  10.5 192.4 %copy-start.7 = (s32[64]{0:T(128)S(1)}, s32[64]{0:T(128)}, u32[]{:S(2)}) copy-start(s32[64]{0:T(128)} %slot_map.3) | copy-start | bytes 772
  10.5 192.4 %copy-start.8 = (s32[16]{0:T(128)S(1)}, s32[16]{0:T(128)}, u32[]{:S(2)}) copy-start(s32[16]{0:T(128)} %get-tuple-element.14.order) | copy-start | bytes 196
  10.5 192.4 %copy-start.9 = (s32[65]{0:T(128)S(1)}, s32[65]{0:T(128)}, u32[]{:S(2)}) copy-start(s32[65]{0:T(128)} %get-tuple-element.15.start) | copy-start | bytes 784
